TPU v7x, 32 devices: a whole 2x2x4 slice. The times are simulated.
32 devices in a mesh: row: 2 (over y), col: 16 (over z, x, core).
Axes of the slice: x: 2, y: 2, z: 4, core: 2. Of those that a mesh axis runs over, the one named last changes fastest.
Arguments:
- matrix: bfloat16 [8192, 8192], P('row', 'col'), may hold values from -6 to 6
- lower_inverse: bfloat16 [2, 1024, 1024], P(None, 'row'), may hold values from -0.03125 to 0.03125
- upper_inverse: bfloat16 [2, 1024, 1024], P(None, 'row'), may hold values from -0.03125 to 0.03125
Outputs:
- factored: bfloat16 [8192, 8192], P('row', 'col')
All inputs are finite; a program needn't handle non-finite values.
Results may differ from a plain program's by a relative error of at most 0.013.
Values may be sent and summed in bfloat16 or wider, within the bound.
A program may use at most 128 MiB of HBM per device.

v0:
```python
import jax
import jax.numpy as jnp
from jax import lax
from jax.sharding import PartitionSpec as P

NB = 1024
STEPS = 2


def spread(value, axis, root):
    mine = lax.axis_index(axis) == root
    return lax.psum(jnp.where(mine, value, jnp.zeros_like(value)), axis)


def shards(matrix, lower_inverse, upper_inverse):
    rows_local, cols_local = matrix.shape
    row_index = lax.axis_index("row")
    col_index = lax.axis_index("col")
    global_rows = row_index * rows_local + jnp.arange(rows_local, dtype=jnp.int32)[:, None]
    global_cols = col_index * cols_local + jnp.arange(cols_local, dtype=jnp.int32)[None, :]
    col_width = min(cols_local, NB)
    current = matrix
    for step_index in range(STEPS):
        block_low = step_index * NB
        block_high = block_low + NB
        owner_row = block_low // rows_local
        row_offset = block_low % rows_local
        source_rows = current[row_offset : row_offset + NB, :]
        is_owner = row_index == owner_row
        lower_full = lax.all_gather(lower_inverse[step_index], "row", axis=0, tiled=True)
        local_top = jnp.dot(lower_full, source_rows, preferred_element_type=jnp.float32).astype(
            jnp.bfloat16
        )
        masked_top = jnp.where(is_owner, local_top.astype(jnp.float32), jnp.float32(0.0))
        top_share = lax.psum_scatter(
            masked_top.astype(jnp.bfloat16), "row", scatter_dimension=0, tiled=True
        )
        top_factor = lax.all_gather(top_share, "row", axis=0, tiled=True)
        upper_start = jnp.clip(col_index * cols_local - block_low, 0, NB - col_width)
        coupling_piece = jnp.dot(
            upper_inverse[step_index], top_factor, preferred_element_type=jnp.float32
        ).astype(jnp.bfloat16)
        coupling = lax.all_gather(coupling_piece, "row", axis=0, tiled=True)
        upper_part = lax.dynamic_slice_in_dim(upper_inverse[step_index], upper_start, col_width, 1)
        upper_cols = lax.all_gather(upper_part, "row", axis=0, tiled=True)
        members = NB // cols_local
        first_root = block_low // cols_local
        panel_source = current
        panel_slabs = [
            spread(panel_source, "col", first_root + member) for member in range(members)
        ]
        whole_panel = jnp.concatenate(panel_slabs, axis=1)
        product = jnp.dot(whole_panel, coupling, preferred_element_type=jnp.float32)
        factor_sum = jnp.dot(whole_panel, upper_cols, preferred_element_type=jnp.float32)
        trailing = (current.astype(jnp.float32) - product).astype(jnp.bfloat16)
        column_factor = factor_sum.astype(jnp.bfloat16)
        placed_rows = lax.dynamic_update_slice(current, top_factor, (row_offset, 0))
        below_block = global_rows >= block_high
        right_block = global_cols >= block_high
        inside_cols = (global_cols >= block_low) & (global_cols < block_high)
        inside_rows = (global_rows >= block_low) & (global_rows < block_high)
        updated = jnp.where(below_block & right_block, trailing, current)
        updated = jnp.where(below_block & inside_cols, column_factor, updated)
        updated = jnp.where(inside_rows & right_block, placed_rows, updated)
        current = updated
    return current


def solution(mesh):
    placed = (P("row", "col"), P(None, "row", None), P(None, "row", None))
    return jax.shard_map(
        shards, mesh=mesh, in_specs=placed, out_specs=P("row", "col"), check_vma=False
    )
```

profile of v0, /device:TPU:29, one launch (start us, length us, event | category | flops | bytes accessed | tf_op | source)
XLA Modules:
  0.0 525.6 jit_solution(9923696612028410579)
XLA Ops:
  7.4 3.0 fusion.42
  10.4 0.0 all-gather.21.cloned.1.call-update
  10.4 0.0 reduce-scatter.3.cloned.1.call-start
  10.5 33.2 %all-gather.21.cloned.1.call-done = bf16[1,1024,1024]{2,1,0:T(8,128)(2,1)} async-done(((bf16[1,512,1024]{2,1,0:T(8,128)(2,1)}), bf16[1,1024,1024]{2,1,0:T(8,128)(2,1)}) %all-gather.21.cloned.1.call-update) | async-done | bytes 2097168 | tf_op jit(solution)/shard_map/all_gather | solution.py:30
  43.7 4.1 select_convert_fusion.1
  47.8 0.0 reduce-scatter.3.cloned.1.call-update
  47.8 0.0 all-gather.13.cloned.1.call-start
  47.9 20.4 %reduce-scatter.3.cloned.1.call-done = bf16[512,512]{1,0:T(8,128)(2,1)} async-done(((bf16[1024,512]{1,0:T(8,128)(2,1)}), bf16[512,512]{1,0:T(8,128)(2,1)}) %reduce-scatter.3.cloned.1.call-update) | async-done | bytes 524304 | tf_op jit(solution)/shard_map/reduce_scatter | solution.py:35
  68.3 0.0 all-gather.13.cloned.1.call-update
  68.3 0.0 all-reduce.7.cloned.1.call-start
  68.4 6.0 %broadcast_select_fusion.2 = (bf16[4096,512]{1,0:T(8,128)(2,1)}, bf16[4096,512]{1,0:T(8,128)(2,1)}) fusion(bf16[4096,512]{1,0:T(8,128)(2,1)} %param.3, pred[]{:T(512)S(6)} %eq.18, pred[]{:T(512)S(6)} %eq.17), kind=kLoop, calls=%fused_computation.12 | loop fusion | flops 4194304 | bytes 12582914 | tf_op jit(solution)/shard_map/jit(_where)/select_n | solution.py:12
  74.4 0.0 all-reduce.7.cloned.1.call-update
  74.4 0.0 all-gather.23.cloned.1.call-start
  74.5 1.5 copy-done.2
  76.0 0.2 fusion.41
  76.1 1.1 constant_dynamic-slice_fusion.1
  77.2 0.0 all-gather.23.cloned.1.call-update
  77.3 0.0 all-gather.15.cloned.1.call-start
  77.3 13.9 %all-gather.13.cloned.1.call-done = bf16[1024,512]{1,0:T(8,128)(2,1)} async-done(((bf16[512,512]{1,0:T(8,128)(2,1)}), bf16[1024,512]{1,0:T(8,128)(2,1)}) %all-gather.13.cloned.1.call-update) | async-done | bytes 1048592 | tf_op jit(solution)/shard_map/all_gather | solution.py:38
  91.3 2.8 fusion.17
  94.1 0.0 all-gather.15.cloned.1.call-update
  94.1 0.0 all-gather.25.cloned.1.call-start
  94.1 0.5 all-gather.25.cloned.1.call-update
  94.7 0.2 reduce-scatter.5.cloned.1.call-start
  94.9 4.5 copy.6
  99.4 145.1 %all-reduce.7.cloned.1.call-done = (bf16[4096,512]{1,0:T(8,128)(2,1)}, bf16[4096,512]{1,0:T(8,128)(2,1)}) async-done(((bf16[4096,512]{1,0:T(8,128)(2,1)}, bf16[4096,512]{1,0:T(8,128)(2,1)}), (bf16[4096,512]{1,0:T(8,128)(2,1)}, bf16[4096,512]{1,0:T(8,128)(2,1)})) %all-reduce.7.cloned.1.call-update) | async-done | bytes 8388624 | tf_op jit(solution)/shard_map/psum | solution.py:12
  244.5 4.7 constant_dynamic-update-slice_fusion.1
  249.2 2.4 constant_dynamic-update-slice_fusion
  251.6 10.3 %convolution_convert_fusion.1 = bf16[4096,512]{1,0:T(8,128)(2,1)} fusion(bf16[4096,1024]{1,0:T(8,128)(2,1)} %constant_dynamic-update-slice_fusion, bf16[1,1024,512]{2,1,0:T(8,128)(2,1)} %all-gather.23.cloned.1.call-done), kind=kOutput, calls=%fused_computation.9 | convolution fusion | flops 4297064448 | bytes 13631488 | tf_op jit(solution)/shard_map/dot_general | solution.py:54
  261.9 1.0 constant_dynamic-update-slice_fusion.5
  262.9 20.6 %broadcast_select_fusion = (bf16[4096,512]{1,0:T(8,128)(2,1)}, bf16[4096,512]{1,0:T(8,128)(2,1)}, bf16[4096,512]{1,0:T(8,128)(2,1)}) fusion(pred[]{:T(512)S(6)} %eq.20, pred[]{:T(512)S(6)} %eq.19, bf16[4096,512]{1,0:T(8,128)(2,1)} %constant_dynamic-update-slice_fusion.5, bf16[4096,512]{1,0:T(8,128)(2,1)} %convolution_convert_fusion.1, ...), kind=kOutput, calls=%fused_computation.10 | convolution fusion | flops 4318035968 | bytes 34612224 | tf_op jit(solution)/shard_map/dot_general | solution.py:53
  283.6 4.1 fusion.12
  287.6 0.0 all-gather.17.cloned.1.call-start
  287.7 20.4 %reduce-scatter.5.cloned.1.call-done = bf16[512,512]{1,0:T(8,128)(2,1)} async-done(((bf16[1024,512]{1,0:T(8,128)(2,1)}), bf16[512,512]{1,0:T(8,128)(2,1)}) %reduce-scatter.5.cloned.1.call-update) | async-done | bytes 524304 | tf_op jit(solution)/shard_map/reduce_scatter | solution.py:35
  308.1 0.0 all-reduce.5.cloned.1.call-start
  308.2 0.5 all-reduce.5.cloned.1.call-update
  308.7 0.0 all-gather.27.cloned.1.call-start
  308.8 1.1 constant_dynamic-slice_fusion
  309.9 0.3 all-gather.19.cloned.1.call-start
  310.2 4.5 copy.10
  314.7 16.3 %all-gather.17.cloned.1.call-done = bf16[1024,512]{1,0:T(8,128)(2,1)} async-done(((bf16[512,512]{1,0:T(8,128)(2,1)}), bf16[1024,512]{1,0:T(8,128)(2,1)}) %all-gather.17.cloned.1.call-update) | async-done | bytes 1048592 | tf_op jit(solution)/shard_map/all_gather | solution.py:38
  331.1 2.9 fusion.18
  334.0 1.1 constant_dynamic-update-slice_fusion.4
  335.1 147.7 %all-reduce.5.cloned.1.call-done = (bf16[4096,512]{1,0:T(8,128)(2,1)}, bf16[4096,512]{1,0:T(8,128)(2,1)}) async-done(((bf16[4096,512]{1,0:T(8,128)(2,1)}, bf16[4096,512]{1,0:T(8,128)(2,1)}), (bf16[4096,512]{1,0:T(8,128)(2,1)}, bf16[4096,512]{1,0:T(8,128)(2,1)})) %all-reduce.5.cloned.1.call-update) | async-done | bytes 8388624 | tf_op jit(solution)/shard_map/psum | solution.py:12
  482.8 4.7 constant_dynamic-update-slice_fusion.3
  487.5 2.4 constant_dynamic-update-slice_fusion.2
  490.0 10.2 %convolution_convert_fusion = bf16[4096,512]{1,0:T(8,128)(2,1)} fusion(bf16[4096,1024]{1,0:T(8,128)(2,1)} %constant_dynamic-update-slice_fusion.2, bf16[1,1024,512]{2,1,0:T(8,128)(2,1)} %all-gather.27.cloned.1.call-done), kind=kOutput, calls=%fused_computation.8 | convolution fusion | flops 4297064448 | bytes 13631488 | tf_op jit(solution)/shard_map/dot_general | solution.py:54
  500.1 18.0 %and_select_fusion.5 = bf16[4096,512]{1,0:T(8,128)(2,1)} fusion(bf16[4096,512]{1,0:T(8,128)(2,1)} %constant_dynamic-update-slice_fusion.4, pred[512]{0:T(512)(128)(4,1)S(1)} %get-tuple-element.20, pred[4096]{0:T(1024)(128)(4,1)S(1)} %get-tuple-element.23, bf16[4096,512]{1,0:T(8,128)(2,1)} %convolution_convert_fusion, ...), kind=kOutput, calls=%fused_computation.7 | convolution fusion | flops 4313841664 | bytes 26223616 | tf_op jit(solution)/shard_map/dot_general | solution.py:53
  (23 shorter events, 0.1 us)
Async XLA Ops:
  7.4 36.3 %all-gather.21.cloned.1.call-start = ((), (), s32[]{:S(2)}) async-start(), calls=%async_computation.8 | async-start | bytes 3145728 | tf_op jit(solution)/shard_map/all_gather | solution.py:30
  10.4 57.9 %reduce-scatter.3.cloned.1.call-start = ((), (), s32[]{:S(2)}) async-start(), calls=%async_computation.2 | async-start | bytes 1572864 | tf_op jit(solution)/shard_map/reduce_scatter | solution.py:35
  47.8 43.4 %all-gather.13.cloned.1.call-start = ((), (), s32[]{:S(2)}) async-start(), calls=%async_computation.3 | async-start | bytes 1572864 | tf_op jit(solution)/shard_map/all_gather | solution.py:38
  68.3 176.2 %all-reduce.7.cloned.1.call-start = ((), (), s32[]{:S(2)}) async-start(), calls=%async_computation.13 | async-start | bytes 16777216 | tf_op jit(solution)/shard_map/psum | solution.py:12
  74.4 1.6 copy-start.2
  74.4 177.2 %all-gather.23.cloned.1.call-start = ((), (), s32[]{:S(2)}) async-start(), calls=%async_computation.9 | async-start | bytes 1572864 | tf_op jit(solution)/shard_map/all_gather | solution.py:45
  77.3 185.7 %all-gather.15.cloned.1.call-start = ((), (), s32[]{:S(2)}) async-start(), calls=%async_computation.4 | async-start | bytes 1572864 | tf_op jit(solution)/shard_map/all_gather | solution.py:43
  94.1 189.5 %all-gather.25.cloned.1.call-start = ((), (), s32[]{:S(2)}) async-start(), calls=%async_computation.10 | async-start | bytes 3145728 | tf_op jit(solution)/shard_map/all_gather | solution.py:30
  94.7 213.5 %reduce-scatter.5.cloned.1.call-start = ((), (), s32[]{:S(2)}) async-start(), calls=%async_computation.5 | async-start | bytes 1572864 | tf_op jit(solution)/shard_map/reduce_scatter | solution.py:35
  244.5 4.8 copy-start
  251.6 10.3 %copy-start.3 = (bf16[1024,512]{1,0:T(8,128)(2,1)S(1)}, bf16[1024,512]{1,0:T(8,128)(2,1)}, u32[]{:S(2)}) copy-start(bf16[1024,512]{1,0:T(8,128)(2,1)} %all-gather.13.cloned.1.call-done) | copy-start | bytes 3145732
  287.6 43.4 %all-gather.17.cloned.1.call-start = ((), (), s32[]{:S(2)}) async-start(), calls=%async_computation.6 | async-start | bytes 1572864 | tf_op jit(solution)/shard_map/all_gather | solution.py:38
  308.1 174.7 %all-reduce.5.cloned.1.call-start = ((), (), s32[]{:S(2)}) async-start(), calls=%async_computation.12 | async-start | bytes 16777216 | tf_op jit(solution)/shard_map/psum | solution.py:12
  308.7 181.2 %all-gather.27.cloned.1.call-start = ((), (), s32[]{:S(2)}) async-start(), calls=%async_computation.11 | async-start | bytes 1572864 | tf_op jit(solution)/shard_map/all_gather | solution.py:45
  309.9 190.2 %all-gather.19.cloned.1.call-start = ((), (), s32[]{:S(2)}) async-start(), calls=%async_computation.7 | async-start | bytes 1572864 | tf_op jit(solution)/shard_map/all_gather | solution.py:43
  331.1 2.9 copy-start.4
  482.8 4.8 copy-start.1
Sparse Core Ops, SparseCore 0:
  10.5 33.1 all-gather.20
  47.9 20.3 reduce-scatter.2
  69.9 21.3 all-gather.12
  92.7 21.3 all-gather.22
  115.4 21.3 all-gather.14
  138.2 33.1 all-gather.24
  287.8 20.3 reduce-scatter.4
  309.7 21.2 all-gather.16
  332.6 21.3 all-gather.26
  355.4 21.3 all-gather.18
Sparse Core Ops, SparseCore 1:
  74.5 169.9 all-reduce.6
  312.9 169.8 all-reduce.4
where the time goes:
time: 529 us; the launch traced here: 526 us
  waiting for transfers between devices  398 us (75%)
  matrix products  72.9 us (14%)
  local copies, waits for them, and re-layouts  32.4 us (6%)
  between operations  15.1 us (3%)
  other arithmetic  6.07 us (1%)
    psum x2, waiting for transfers between devices, spread(): return lax.psum(jnp.where(mine, value, jnp.zeros_like(value)), axis)  293 us
    reduce_scatter x2, waiting for transfers between devices, shards(): lax.psum_scatter(masked_top.astype(jnp.bfloat16), 'row', scatter_dimensio...  40.8 us
    dot_general x2, matrix products, shards(): product = jnp.dot(whole_panel, coupling, preferred_element_type=jnp.float32)  38.6 us
    all_gather x2, waiting for transfers between devices, shards(): lax.all_gather(lower_inverse[step_index], 'row', axis=0, tiled=True)  33.2 us
    all_gather x2, waiting for transfers between devices, shards(): top_factor = lax.all_gather(top_share, 'row', axis=0, tiled=True)  30.3 us
    dot_general x2, matrix products, shards(): jnp.dot(whole_panel, upper_cols, preferred_element_type=jnp.float32)  20.4 us
    unnamed x14, local copies, waits for them, and re-layouts  20 us
  transfers between devices with their start and end apart: 12, of which 7 were waited for; matrix products, arithmetic and copies ran while one was open for 15% of the time, Pallas kernels for 0%

commit v1 on v0

--- a/solution.py
+++ b/solution.py
@@ -1,6 +1,10 @@
+import functools
+
 import jax
 import jax.numpy as jnp
 from jax import lax
+from jax.experimental import pallas as pl
+from jax.experimental.pallas import tpu as pltpu
 from jax.sharding import PartitionSpec as P
 
 NB = 1024
@@ -66,8 +70,356 @@
     return current
 
 
+CHUNK = 128
+PER = 4
+BLOCK = CHUNK * PER
+MESH = pl.DeviceIdType.MESH
+
+
+def both(*terms):
+    out = terms[0]
+    for term in terms[1:]:
+        out = jnp.logical_and(out, term)
+    return out
+
+
+def fused(depth, m, lo, up, out, panel, lower_in, upper_in, factor, rows_done, own, par,
+          z_sent, x_sent, c_sent, r_sent, ex_y, ex_c, ex_y_sent, ex_c_sent, f_in, f_sent):
+    y = lax.axis_index("row")
+    col = lax.axis_index("col")
+    c = lax.rem(col, 2)
+    x = lax.rem(col // 2, 2)
+    z = col // 4
+    width = m.shape[1]
+    half = NB // 2
+    quarter = half // 2
+    up_z, down_z = col + 4, col - 4
+    other_x = col + 2 - 4 * x
+    other_c = col + 1 - 2 * c
+    first = both(z == 0, x == 0)
+    second = both(z == 0, x == 1)
+    offset = NB * (1 - y)
+    n_a = m.shape[0] // BLOCK - (NB // BLOCK) * (1 - y)
+    start_b = (NB // BLOCK) * (1 - y)
+    n_b = n_a - start_b
+
+    barrier = pltpu.get_barrier_semaphore()
+
+    def greet(target_y, target):
+        pl.semaphore_signal(barrier, inc=1, device_id=(target_y, target), device_id_type=MESH)
+
+    greet(1 - y, col)
+    greet(y, other_x)
+    greet(y, other_c)
+
+    @pl.when(z > 0)
+    def _():
+        greet(y, down_z)
+
+    @pl.when(z < depth - 1)
+    def _():
+        greet(y, up_z)
+
+    ends = jnp.where(z == 0, 1, 0) + jnp.where(z == depth - 1, 1, 0)
+    pl.semaphore_wait(barrier, 5 - ends)
+
+    def row_of(b):
+        return pl.multiple_of(offset + b * BLOCK, BLOCK)
+
+    def piece(s, which, b, i):
+        return panel.at[s, which, pl.ds(pl.multiple_of(row_of(b) + i * CHUNK, CHUNK), CHUNK), :]
+
+    def send(s, b, i, target, sent, landed):
+        ref = piece(s, c, b, i)
+        return pltpu.make_async_remote_copy(
+            src_ref=ref, dst_ref=ref, send_sem=sent.at[i], recv_sem=landed.at[s, b * PER + i],
+            device_id=(y, target), device_id_type=MESH)
+
+    def arrived(s, which, b, i, landed, sent):
+        ref = piece(s, which, b, i)
+        pltpu.make_async_remote_copy(
+            src_ref=ref, dst_ref=ref, send_sem=sent.at[i], recv_sem=landed.at[s, b * PER + i],
+            device_id=(y, other_c), device_id_type=MESH).wait_recv()
+
+    def sends(s, b, i, begin):
+        odd = i % 2
+        act = (lambda d: d.start()) if begin else (lambda d: d.wait_send())
+
+        @pl.when(both(z < depth - 1, x == odd))
+        def _():
+            act(send(s, b, i, up_z, z_sent, own))
+
+        across = both(z > 0, x == odd)
+        if s == 0 and odd == 1:
+            across = jnp.logical_or(across, first)
+        if s == 1 and odd == 0:
+            across = jnp.logical_or(across, second)
+
+        @pl.when(across)
+        def _():
+            act(send(s, b, i, other_x, x_sent, own))
+
+        if s == 0 and odd == 0:
+            @pl.when(both(z == 1, x == 1))
+            def _():
+                act(send(s, b, i, down_z, r_sent, own))
+
+        if s == 0:
+            act(send(s, b, i, other_c, c_sent, par))
+        else:
+            @pl.when(jnp.logical_not(first))
+            def _():
+                act(send(s, b, i, other_c, c_sent, par))
+
+    def relay(s, b, begin_b):
+        for i in range(PER):
+            if s == 0:
+                need = jnp.logical_not(first)
+            elif i % 2 == 0:
+                need = jnp.logical_not(second)
+            else:
+                need = z > 0
+
+            @pl.when(need)
+            def _():
+                arrived(s, c, b, i, own, c_sent)
+
+            @pl.when(b > begin_b)
+            def _():
+                sends(s, b - 1, i, False)
+
+            sends(s, b, i, True)
+
+    def drain(s, last):
+        for i in range(PER):
+            sends(s, last, i, False)
+
+    def phase_a(b):
+        @pl.when(first)
+        def _():
+            at = pl.ds(row_of(b), BLOCK)
+            panel[0, c, at, :] = m[at, :]
+
+        relay(0, b, 0)
+
+    def product(s, b):
+        at = pl.ds(row_of(b), BLOCK)
+        total = jnp.dot(panel[s, 0, at, :], factor[s, :width, :], preferred_element_type=jnp.float32)
+        return total + jnp.dot(
+            panel[s, 1, at, :], factor[s, width:, :], preferred_element_type=jnp.float32)
+
+    def update_0(b):
+        for i in range(PER):
+            arrived(0, 1 - c, b, i, par, c_sent)
+        at = pl.ds(row_of(b), BLOCK)
+        total = product(0, b)
+        kept = m[at, :].astype(jnp.float32)
+        out[at, :] = jnp.where(first, total, kept - total).astype(out.dtype)
+
+    def update_1(b):
+        @pl.when(jnp.logical_not(first))
+        def _():
+            for i in range(PER):
+                arrived(1, 1 - c, b, i, par, c_sent)
+            at = pl.ds(row_of(b), BLOCK)
+            total = product(1, b)
+            kept = out[at, :].astype(jnp.float32)
+            out[at, :] = jnp.where(second, total, kept - total).astype(out.dtype)
+
+    def inverse_y(item):
+        s = item // 2
+        src = (lo, up)[item % 2]
+        dst = (lower_in, upper_in)[item % 2]
+        at = pl.ds(pl.multiple_of(c * quarter, quarter), quarter)
+        return pltpu.make_async_remote_copy(
+            src_ref=src.at[s, at, :], dst_ref=dst.at[s, at, :], send_sem=ex_y_sent.at[item],
+            recv_sem=ex_y.at[item], device_id=(1 - y, col), device_id_type=MESH)
+
+    def inverse_c(item, which):
+        s = item // 2
+        dst = (lower_in, upper_in)[item % 2]
+        ref = dst.at[s, pl.ds(pl.multiple_of(which * quarter, quarter), quarter), :]
+        return pltpu.make_async_remote_copy(
+            src_ref=ref, dst_ref=ref, send_sem=ex_c_sent.at[item],
+            recv_sem=ex_c.at[item], device_id=(y, other_c), device_id_type=MESH)
+
+    def take_inverse(item):
+        inverse_y(item).wait_recv()
+        inverse_c(item, c).start()
+        inverse_c(item, 1 - c).wait_recv()
+
+    def factor_y(s, part):
+        ref = factor.at[s, pl.ds(part * half, half), :]
+        return pltpu.make_async_remote_copy(
+            src_ref=ref, dst_ref=ref, send_sem=f_sent.at[2 * s + part],
+            recv_sem=f_in.at[2 * s + part], device_id=(1 - y, col), device_id_type=MESH)
+
+    def make_rows(s):
+        src = m if s == 0 else out
+        at = pl.ds(s * NB, NB)
+        rows_done[:half, :] = jnp.dot(
+            lo[s], src[at, :], preferred_element_type=jnp.float32).astype(jnp.bfloat16)
+        rows_done[half:, :] = jnp.dot(
+            lower_in[s], src[at, :], preferred_element_type=jnp.float32).astype(jnp.bfloat16)
+        if s == 0:
+            out[at, :] = jnp.where(first, m[at, :], rows_done[...])
+        else:
+            @pl.when(z * 2 + x > 1)
+            def _():
+                out[at, :] = rows_done[...]
+
+    def make_factor(s, part):
+        src = up if part == 0 else upper_in
+        at = pl.ds(part * half, half)
+        inside = first if s == 0 else second
+
+        @pl.when(jnp.logical_not(inside))
+        def _():
+            factor[s, at, :] = jnp.dot(
+                src[s], rows_done[...], preferred_element_type=jnp.float32).astype(jnp.bfloat16)
+
+        @pl.when(inside)
+        def _():
+            factor[s, at, :] = jnp.where(c == 0, src[s, :, :width], src[s, :, width:])
+
+        factor_y(s, part).start()
+
+    @pl.when(y == 0)
+    def _():
+        phase_a(0)
+        take_inverse(0)
+        make_rows(0)
+        make_factor(0, 0)
+        phase_a(1)
+        take_inverse(1)
+        make_factor(0, 1)
+
+        @pl.loop(0, 2)
+        def _(b):
+            update_0(b)
+            phase_a(b + 2)
+
+        take_inverse(2)
+        make_rows(1)
+        make_factor(1, 0)
+
+        @pl.loop(4, 6)
+        def _(b):
+            phase_a(b)
+
+        take_inverse(3)
+        make_factor(1, 1)
+
+    @pl.when(y == 1)
+    def _():
+        inverse_y(0).start()
+        inverse_y(1).start()
+
+        @pl.loop(0, 3)
+        def _(b):
+            phase_a(b)
+
+        inverse_y(0).wait_send()
+        inverse_y(1).wait_send()
+        inverse_y(2).start()
+        inverse_y(3).start()
+
+        @pl.loop(3, n_a)
+        def _(b):
+            phase_a(b)
+
+        factor_y(0, 0).wait_recv()
+        factor_y(0, 1).wait_recv()
+
+    drain(0, n_a - 1)
+
+    @pl.loop(0, n_b)
+    def _(j):
+        b = start_b + j
+        later = j - n_b // 2
+
+        @pl.when(second)
+        def _():
+            update_0(b)
+            at = pl.ds(row_of(b), BLOCK)
+            panel[1, c, at, :] = out[at, :]
+
+        relay(1, b, start_b)
+
+        @pl.when(both(later < 0, jnp.logical_not(second)))
+        def _():
+            @pl.loop(0, 2)
+            def _(t):
+                update_0(start_b + 2 * j + t)
+
+        @pl.when(both(later == 0, y == 1))
+        def _():
+            factor_y(1, 0).wait_recv()
+            factor_y(1, 1).wait_recv()
+
+        @pl.when(later >= 0)
+        def _():
+            @pl.loop(0, 2)
+            def _(t):
+                update_1(start_b + 2 * later + t)
+
+    drain(1, n_a - 1)
+
+    @pl.when(y == 0)
+    def _():
+        for item in range(4):
+            inverse_c(item, c).wait_send()
+            factor_y(item // 2, item % 2).wait_send()
+
+    @pl.when(y == 1)
+    def _():
+        inverse_y(2).wait_send()
+        inverse_y(3).wait_send()
+
+
+def streamed(depth, matrix, lower_inverse, upper_inverse):
+    rows, width = matrix.shape
+    half = NB // 2
+    chunks = rows // CHUNK
+    dma = pltpu.SemaphoreType.DMA
+    return pl.pallas_call(
+        functools.partial(fused, depth),
+        out_shape=jax.ShapeDtypeStruct((rows, width), jnp.bfloat16),
+        in_specs=[pl.BlockSpec(memory_space=pltpu.VMEM)] * 3,
+        out_specs=pl.BlockSpec(memory_space=pltpu.VMEM),
+        scratch_shapes=[
+            pltpu.VMEM((STEPS, 2, rows, width), jnp.bfloat16),
+            pltpu.VMEM((STEPS, half, NB), jnp.bfloat16),
+            pltpu.VMEM((STEPS, half, NB), jnp.bfloat16),
+            pltpu.VMEM((STEPS, NB, width), jnp.bfloat16),
+            pltpu.VMEM((NB, width), jnp.bfloat16),
+            dma((STEPS, chunks)),
+            dma((STEPS, chunks)),
+            dma((PER,)),
+            dma((PER,)),
+            dma((PER,)),
+            dma((PER,)),
+            dma((4,)),
+            dma((4,)),
+            dma((4,)),
+            dma((4,)),
+            dma((4,)),
+            dma((4,)),
+        ],
+        compiler_params=pltpu.CompilerParams(
+            collective_id=0, has_side_effects=True, vmem_limit_bytes=56 * 1024 * 1024),
+        cost_estimate=pl.CostEstimate(
+            flops=4 * rows * width * NB * STEPS, bytes_accessed=4 * rows * width, transcendentals=0),
+    )(matrix, lower_inverse, upper_inverse)
+
+
+def fits(mesh):
+    return mesh.shape["row"] == 2 and mesh.shape["col"] == 16
+
+
 def solution(mesh):
     placed = (P("row", "col"), P(None, "row", None), P(None, "row", None))
+    body = functools.partial(streamed, mesh.shape["col"] // 4) if fits(mesh) else shards
     return jax.shard_map(
-        shards, mesh=mesh, in_specs=placed, out_specs=P("row", "col"), check_vma=False
+        body, mesh=mesh, in_specs=placed, out_specs=P("row", "col"), check_vma=False
     )

time: 529 us -> 437 us (0.83)
  Pallas kernels: 0 us -> 432 us
  waiting for transfers between devices: 398 us -> 0 us
  matrix products: 72.9 us -> 0 us
  local copies, waits for them, and re-layouts: 32.4 us -> 4.47 us
  between operations: 15.1 us -> 0.01 us
  other arithmetic: 6.07 us -> 0 us
    pallas_call x0 -> x1, Pallas kernels: none -> 432 us  [streamed(): pl.pallas_call(functools.partial(fused, depth), out_shape=jax.ShapeDtypeS...]
    psum x2 -> x0, waiting for transfers between devices: 293 us -> none  [spread(): return lax.psum(jnp.where(mine, value, jnp.zeros_like(value)), axis)]
    dot_general x8 -> x0, matrix products: 72.9 us -> none  [the longest x2 38.6 us: shards(): product = jnp.dot(whole_panel, coupling, preferred_element_type=jnp.float32)]
    all_gather x8 -> x0, waiting for transfers between devices: 63.5 us -> none  [the longest x2 33.2 us: shards(): lax.all_gather(lower_inverse[step_index], 'row', axis=0, tiled=True)]
    reduce_scatter x2 -> x0, waiting for transfers between devices: 40.8 us -> none  [shards(): lax.psum_scatter(masked_top.astype(jnp.bfloat16), 'row', scatter_dimensio...]
    unnamed x14 -> x1, local copies, waits for them, and re-layouts: 20 us -> 4.47 us
    select_n x1 -> x0, other arithmetic: 6.03 us -> none  [spread(): return lax.psum(jnp.where(mine, value, jnp.zeros_like(value)), axis)]
  transfers between devices with their start and end apart: 12 -> 0, of which waited for: 7 -> 0; matrix products, arithmetic and copies ran while one was open for 15% -> 0% of each run, Pallas kernels for 0% -> 0%
where the time goes in v1:
time: 437 us
  Pallas kernels  432 us (99%)
  local copies, waits for them, and re-layouts  4.47 us (1%)
    pallas_call x1, Pallas kernels, streamed(): pl.pallas_call(functools.partial(fused, depth), out_shape=jax.ShapeDtypeS...  432 us

profile of v1, /device:TPU:29, one launch (start us, length us, event | category | flops | bytes accessed | tf_op | source)
XLA Modules:
  0.0 436.7 jit_solution(12522587665500242883)
XLA Ops:
  0.0 432.2 %shard_map.37 = bf16[4096,512]{1,0:T(8,128)(2,1)} custom-call(bf16[4096,512]{1,0:T(8,128)(2,1)} %m.1, bf16[2,512,1024]{2,1,0:T(8,128)(2,1)} %lo.1, bf16[2,512,1024]{2,1,0:T(8,128)(2,1)} %up.1), custom_call_target="tpu_custom_call" | custom-call | flops 17179869184 | bytes 8388608 | tf_op jit(solution)/shard_map/pallas_call | solution.py:385
  432.3 4.5 %copy.5 = bf16[4096,512]{1,0:T(8,128)(2,1)} copy(bf16[4096,512]{1,0:T(8,128)(2,1)} %shard_map.37) | data formatting | bytes 8388608

commit v2 on v1

--- a/solution.py
+++ b/solution.py
@@ -132,75 +132,101 @@
     def send(s, b, i, target, sent, landed):
         ref = piece(s, c, b, i)
         return pltpu.make_async_remote_copy(
-            src_ref=ref, dst_ref=ref, send_sem=sent.at[i], recv_sem=landed.at[s, b * PER + i],
+            src_ref=ref, dst_ref=ref, send_sem=sent, recv_sem=landed.at[s, b * PER + i],
             device_id=(y, target), device_id_type=MESH)
 
-    def arrived(s, which, b, i, landed, sent):
+    def arrived(s, which, b, i, landed):
         ref = piece(s, which, b, i)
         pltpu.make_async_remote_copy(
-            src_ref=ref, dst_ref=ref, send_sem=sent.at[i], recv_sem=landed.at[s, b * PER + i],
+            src_ref=ref, dst_ref=ref, send_sem=c_sent.at[0, 0], recv_sem=landed.at[s, b * PER + i],
             device_id=(y, other_c), device_id_type=MESH).wait_recv()
 
-    def sends(s, b, i, begin):
-        odd = i % 2
-        act = (lambda d: d.start()) if begin else (lambda d: d.wait_send())
-
-        @pl.when(both(z < depth - 1, x == odd))
-        def _():
-            act(send(s, b, i, up_z, z_sent, own))
-
-        across = both(z > 0, x == odd)
-        if s == 0 and odd == 1:
-            across = jnp.logical_or(across, first)
-        if s == 1 and odd == 0:
-            across = jnp.logical_or(across, second)
-
-        @pl.when(across)
-        def _():
-            act(send(s, b, i, other_x, x_sent, own))
-
-        if s == 0 and odd == 0:
+    def begin(d):
+        d.start()
+
+    def finish(d):
+        d.wait_send()
+
+    def source(s):
+        return first if s == 0 else second
+
+    def chain_sends(s, b, t, act):
+        i = 2 * t + x
+        slot = lax.rem(b, 2) * 2 + t
+
+        @pl.when(z < depth - 1)
+        def _():
+            act(send(s, b, i, up_z, z_sent.at[slot], own))
+
+        @pl.when(z > 0)
+        def _():
+            act(send(s, b, i, other_x, x_sent.at[slot], own))
+
+        @pl.when(jnp.logical_not(first) if s == 1 else True)
+        def _():
+            act(send(s, b, i, other_c, c_sent.at[0, slot], par))
+
+    def cross_sends(s, b, t, act):
+        i = 2 * t + 1 - x
+        slot = lax.rem(b, 2) * 2 + t
+
+        @pl.when(source(s))
+        def _():
+            act(send(s, b, i, other_x, x_sent.at[slot], own))
+
+        if s == 0:
             @pl.when(both(z == 1, x == 1))
             def _():
-                act(send(s, b, i, down_z, r_sent, own))
-
-        if s == 0:
-            act(send(s, b, i, other_c, c_sent, par))
-        else:
-            @pl.when(jnp.logical_not(first))
-            def _():
-                act(send(s, b, i, other_c, c_sent, par))
-
-    def relay(s, b, begin_b):
-        for i in range(PER):
-            if s == 0:
-                need = jnp.logical_not(first)
-            elif i % 2 == 0:
-                need = jnp.logical_not(second)
-            else:
-                need = z > 0
-
-            @pl.when(need)
-            def _():
-                arrived(s, c, b, i, own, c_sent)
-
-            @pl.when(b > begin_b)
-            def _():
-                sends(s, b - 1, i, False)
-
-            sends(s, b, i, True)
+                act(send(s, b, i, down_z, r_sent.at[slot], own))
+
+        act(send(s, b, i, other_c, c_sent.at[1, slot], par))
+
+    def chain(s, b, begin_b):
+        for t in range(2):
+            @pl.when(jnp.logical_not(source(s)))
+            def _():
+                arrived(s, c, b, 2 * t + x, own)
+
+            @pl.when(b >= begin_b + 2)
+            def _():
+                chain_sends(s, b - 2, t, finish)
+
+            chain_sends(s, b, t, begin)
+
+    def cross(s, b, begin_b):
+        for t in range(2):
+            @pl.when(jnp.logical_not(source(s)))
+            def _():
+                arrived(s, c, b, 2 * t + 1 - x, own)
+
+            @pl.when(b >= begin_b + 2)
+            def _():
+                cross_sends(s, b - 2, t, finish)
+
+            cross_sends(s, b, t, begin)
 
     def drain(s, last):
-        for i in range(PER):
-            sends(s, last, i, False)
-
-    def phase_a(b):
-        @pl.when(first)
-        def _():
-            at = pl.ds(row_of(b), BLOCK)
-            panel[0, c, at, :] = m[at, :]
-
-        relay(0, b, 0)
+        for b in (last - 1, last):
+            for t in range(2):
+                chain_sends(s, b, t, finish)
+
+                @pl.when(jnp.logical_not(first) if s == 1 else True)
+                def _():
+                    cross_sends(s, b, t, finish)
+
+    def phase_a(b, lag):
+        @pl.when(b < n_a)
+        def _():
+            @pl.when(first)
+            def _():
+                at = pl.ds(row_of(b), BLOCK)
+                panel[0, c, at, :] = m[at, :]
+
+            chain(0, b, 0)
+
+        @pl.when(both(b >= lag, b < n_a + lag))
+        def _():
+            cross(0, b - lag, 0)
 
     def product(s, b):
         at = pl.ds(row_of(b), BLOCK)
@@ -210,7 +236,7 @@
 
     def update_0(b):
         for i in range(PER):
-            arrived(0, 1 - c, b, i, par, c_sent)
+            arrived(0, 1 - c, b, i, par)
         at = pl.ds(row_of(b), BLOCK)
         total = product(0, b)
         kept = m[at, :].astype(jnp.float32)
@@ -220,7 +246,7 @@
         @pl.when(jnp.logical_not(first))
         def _():
             for i in range(PER):
-                arrived(1, 1 - c, b, i, par, c_sent)
+                arrived(1, 1 - c, b, i, par)
             at = pl.ds(row_of(b), BLOCK)
             total = product(1, b)
             kept = out[at, :].astype(jnp.float32)
@@ -286,82 +312,96 @@
 
     @pl.when(y == 0)
     def _():
-        phase_a(0)
+        lag = jnp.where(first, 0, 2)
+
+        @pl.loop(0, 2)
+        def _(b):
+            phase_a(b, lag)
+
         take_inverse(0)
         make_rows(0)
         make_factor(0, 0)
-        phase_a(1)
+        phase_a(jnp.int32(2), lag)
         take_inverse(1)
         make_factor(0, 1)
+        phase_a(jnp.int32(3), lag)
 
         @pl.loop(0, 2)
         def _(b):
             update_0(b)
-            phase_a(b + 2)
-
+
+        phase_a(jnp.int32(4), lag)
         take_inverse(2)
         make_rows(1)
         make_factor(1, 0)
 
-        @pl.loop(4, 6)
+        @pl.loop(5, 8)
         def _(b):
-            phase_a(b)
+            phase_a(b, lag)
 
         take_inverse(3)
         make_factor(1, 1)
 
     @pl.when(y == 1)
     def _():
+        lag = jnp.where(first, 0, jnp.where(second, 4, 2))
         inverse_y(0).start()
         inverse_y(1).start()
 
-        @pl.loop(0, 3)
+        @pl.loop(0, n_a + 4)
         def _(b):
-            phase_a(b)
-
-        inverse_y(0).wait_send()
-        inverse_y(1).wait_send()
-        inverse_y(2).start()
-        inverse_y(3).start()
-
-        @pl.loop(3, n_a)
-        def _(b):
-            phase_a(b)
+            phase_a(b, lag)
+
+            @pl.when(b == 3)
+            def _():
+                inverse_y(0).wait_send()
+                inverse_y(1).wait_send()
+                inverse_y(2).start()
+                inverse_y(3).start()
 
         factor_y(0, 0).wait_recv()
         factor_y(0, 1).wait_recv()
 
     drain(0, n_a - 1)
-
-    @pl.loop(0, n_b)
+    half_b = n_b // 2
+    lag_b = jnp.where(second, 0, 2)
+
+    @pl.loop(0, n_b + 2)
     def _(j):
         b = start_b + j
-        later = j - n_b // 2
-
-        @pl.when(second)
-        def _():
-            update_0(b)
-            at = pl.ds(row_of(b), BLOCK)
-            panel[1, c, at, :] = out[at, :]
-
-        relay(1, b, start_b)
-
-        @pl.when(both(later < 0, jnp.logical_not(second)))
+
+        @pl.when(j < n_b)
+        def _():
+            @pl.when(second)
+            def _():
+                update_0(b)
+                at = pl.ds(row_of(b), BLOCK)
+                panel[1, c, at, :] = out[at, :]
+
+            chain(1, b, start_b)
+
+        @pl.when(both(jnp.logical_not(first), j >= lag_b, j < n_b + lag_b))
+        def _():
+            cross(1, b - lag_b, start_b)
+
+        @pl.when(both(j < half_b, jnp.logical_not(second)))
         def _():
             @pl.loop(0, 2)
             def _(t):
                 update_0(start_b + 2 * j + t)
 
-        @pl.when(both(later == 0, y == 1))
+        @pl.when(both(j == half_b, y == 1))
         def _():
             factor_y(1, 0).wait_recv()
             factor_y(1, 1).wait_recv()
 
-        @pl.when(later >= 0)
-        def _():
-            @pl.loop(0, 2)
+        @pl.when(j >= half_b)
+        def _():
+            low = jnp.where(j == half_b, 0, j - 2)
+
+            @pl.loop(0, j - 1 - low)
             def _(t):
-                update_1(start_b + 2 * later + t)
+                update_1(start_b + low + t)
 
     drain(1, n_a - 1)
 
@@ -397,7 +437,7 @@
             dma((STEPS, chunks)),
             dma((PER,)),
             dma((PER,)),
-            dma((PER,)),
+            dma((2, PER)),
             dma((PER,)),
             dma((4,)),
             dma((4,)),

time: 437 us -> 168 us (0.38)
  Pallas kernels: 432 us -> 164 us
    pallas_call x1, Pallas kernels: 432 us -> 164 us  [streamed(): pl.pallas_call(functools.partial(fused, depth), out_shape=jax.ShapeDtypeS...]
where the time goes in v2:
time: 168 us
  Pallas kernels  164 us (98%)
  local copies, waits for them, and re-layouts  4.47 us (3%)
    pallas_call x1, Pallas kernels, streamed(): pl.pallas_call(functools.partial(fused, depth), out_shape=jax.ShapeDtypeS...  164 us
    unnamed x1, local copies, waits for them, and re-layouts  4.47 us

profile of v2, /device:TPU:29, one launch (start us, length us, event | category | flops | bytes accessed | tf_op | source)
XLA Modules:
  0.0 168.0 jit_solution(710419515402987875)
XLA Ops:
  0.0 163.5 %shard_map.37 = bf16[4096,512]{1,0:T(8,128)(2,1)} custom-call(bf16[4096,512]{1,0:T(8,128)(2,1)} %m.1, bf16[2,512,1024]{2,1,0:T(8,128)(2,1)} %lo.1, bf16[2,512,1024]{2,1,0:T(8,128)(2,1)} %up.1), custom_call_target="tpu_custom_call" | custom-call | flops 17179869184 | bytes 8388608 | tf_op jit(solution)/shard_map/pallas_call | solution.py:425
  163.6 4.5 %copy.5 = bf16[4096,512]{1,0:T(8,128)(2,1)} copy(bf16[4096,512]{1,0:T(8,128)(2,1)} %shard_map.37) | data formatting | bytes 8388608

commit v3 on v2

--- a/solution.py
+++ b/solution.py
@@ -314,17 +314,26 @@
     def _():
         lag = jnp.where(first, 0, 2)
 
-        @pl.loop(0, 2)
-        def _(b):
-            phase_a(b, lag)
+        phase_a(jnp.int32(0), lag)
+
+        @pl.when(z == 0)
+        def _():
+            phase_a(jnp.int32(1), lag)
 
         take_inverse(0)
         make_rows(0)
         make_factor(0, 0)
-        phase_a(jnp.int32(2), lag)
+
+        @pl.when(z > 0)
+        def _():
+            phase_a(jnp.int32(1), lag)
+
         take_inverse(1)
         make_factor(0, 1)
-        phase_a(jnp.int32(3), lag)
+
+        @pl.loop(2, 4)
+        def _(b):
+            phase_a(b, lag)
 
         @pl.loop(0, 2)
         def _(b):
@@ -346,18 +355,17 @@
     def _():
         lag = jnp.where(first, 0, jnp.where(second, 4, 2))
         inverse_y(0).start()
-        inverse_y(1).start()
+        hold = jnp.where(z == 0, 2, 0)
 
         @pl.loop(0, n_a + 4)
         def _(b):
             phase_a(b, lag)
 
-            @pl.when(b == 3)
-            def _():
-                inverse_y(0).wait_send()
-                inverse_y(1).wait_send()
-                inverse_y(2).start()
-                inverse_y(3).start()
+            for item in range(1, 4):
+                @pl.when(b == hold + 2 * (item - 1))
+                def _():
+                    inverse_y(item - 1).wait_send()
+                    inverse_y(item).start()
 
         factor_y(0, 0).wait_recv()
         factor_y(0, 1).wait_recv()
@@ -413,7 +421,6 @@
 
     @pl.when(y == 1)
     def _():
-        inverse_y(2).wait_send()
         inverse_y(3).wait_send()
 
 

time: 168 us -> 177 us (1.054)
  Pallas kernels: 164 us -> 172 us
    pallas_call x1, Pallas kernels: 164 us -> 172 us  [streamed(): pl.pallas_call(functools.partial(fused, depth), out_shape=jax.ShapeDtypeS...]
where the time goes in v3:
time: 177 us; the launch traced here: 176 us
  Pallas kernels  172 us (97%)
  local copies, waits for them, and re-layouts  4.47 us (3%)
    pallas_call x1, Pallas kernels, streamed(): pl.pallas_call(functools.partial(fused, depth), out_shape=jax.ShapeDtypeS...  172 us
    unnamed x1, local copies, waits for them, and re-layouts  4.47 us

profile of v3, /device:TPU:29, one launch (start us, length us, event | category | flops | bytes accessed | tf_op | source)
XLA Modules:
  0.0 176.3 jit_solution(465425539123029509)
XLA Ops:
  0.0 171.8 %shard_map.37 = bf16[4096,512]{1,0:T(8,128)(2,1)} custom-call(bf16[4096,512]{1,0:T(8,128)(2,1)} %m.1, bf16[2,512,1024]{2,1,0:T(8,128)(2,1)} %lo.1, bf16[2,512,1024]{2,1,0:T(8,128)(2,1)} %up.1), custom_call_target="tpu_custom_call" | custom-call | flops 17179869184 | bytes 8388608 | tf_op jit(solution)/shard_map/pallas_call | solution.py:432
  171.8 4.5 %copy.5 = bf16[4096,512]{1,0:T(8,128)(2,1)} copy(bf16[4096,512]{1,0:T(8,128)(2,1)} %shard_map.37) | data formatting | bytes 8388608

commit v4 on v2

--- a/solution.py
+++ b/solution.py
@@ -287,19 +287,14 @@
             lo[s], src[at, :], preferred_element_type=jnp.float32).astype(jnp.bfloat16)
         rows_done[half:, :] = jnp.dot(
             lower_in[s], src[at, :], preferred_element_type=jnp.float32).astype(jnp.bfloat16)
-        if s == 0:
-            out[at, :] = jnp.where(first, m[at, :], rows_done[...])
-        else:
-            @pl.when(z * 2 + x > 1)
-            def _():
-                out[at, :] = rows_done[...]
+        out[at, :] = rows_done[...]
 
     def make_factor(s, part):
         src = up if part == 0 else upper_in
         at = pl.ds(part * half, half)
-        inside = first if s == 0 else second
-
-        @pl.when(jnp.logical_not(inside))
+        inside = source(s)
+
+        @pl.when(jnp.logical_not(jnp.logical_or(first, inside)))
         def _():
             factor[s, at, :] = jnp.dot(
                 src[s], rows_done[...], preferred_element_type=jnp.float32).astype(jnp.bfloat16)
@@ -308,43 +303,60 @@
         def _():
             factor[s, at, :] = jnp.where(c == 0, src[s, :, :width], src[s, :, width:])
 
-        factor_y(s, part).start()
+        @pl.when(jnp.logical_not(first) if s == 1 else True)
+        def _():
+            factor_y(s, part).start()
 
     @pl.when(y == 0)
     def _():
-        lag = jnp.where(first, 0, 2)
-
-        @pl.loop(0, 2)
+        lag = jnp.where(first, 0, jnp.where(second, 3, 2))
+        ahead = jnp.where(first, n_a, jnp.where(z == 0, 3, 2))
+        middle = jnp.maximum(ahead, 2 + lag)
+
+        @pl.loop(0, ahead)
         def _(b):
             phase_a(b, lag)
 
         take_inverse(0)
-        make_rows(0)
+
+        @pl.when(jnp.logical_not(first))
+        def _():
+            make_rows(0)
+
+        @pl.when(first)
+        def _():
+            out[:NB, :] = m[:NB, :]
+
         make_factor(0, 0)
-        phase_a(jnp.int32(2), lag)
         take_inverse(1)
         make_factor(0, 1)
-        phase_a(jnp.int32(3), lag)
+
+        @pl.loop(0, middle - ahead)
+        def _(t):
+            phase_a(ahead + t, lag)
 
         @pl.loop(0, 2)
         def _(b):
             update_0(b)
 
-        phase_a(jnp.int32(4), lag)
+        @pl.loop(0, n_a + lag - middle)
+        def _(t):
+            phase_a(middle + t, lag)
+
         take_inverse(2)
-        make_rows(1)
+
+        @pl.when(z * 2 + x > 1)
+        def _():
+            make_rows(1)
+
         make_factor(1, 0)
-
-        @pl.loop(5, 8)
-        def _(b):
-            phase_a(b, lag)
-
         take_inverse(3)
         make_factor(1, 1)
 
     @pl.when(y == 1)
     def _():
         lag = jnp.where(first, 0, jnp.where(second, 4, 2))
+        hold = jnp.where(z == 0, 3, 1)
         inverse_y(0).start()
         inverse_y(1).start()
 
@@ -352,7 +364,7 @@
         def _(b):
             phase_a(b, lag)
 
-            @pl.when(b == 3)
+            @pl.when(b == hold)
             def _():
                 inverse_y(0).wait_send()
                 inverse_y(1).wait_send()
@@ -364,6 +376,7 @@
 
     drain(0, n_a - 1)
     half_b = n_b // 2
+    turn = half_b + y
     lag_b = jnp.where(second, 0, 2)
 
     @pl.loop(0, n_b + 2)
@@ -390,16 +403,17 @@
             def _(t):
                 update_0(start_b + 2 * j + t)
 
-        @pl.when(both(j == half_b, y == 1))
+        @pl.when(both(j == turn, y == 1, jnp.logical_not(first)))
         def _():
             factor_y(1, 0).wait_recv()
             factor_y(1, 1).wait_recv()
 
-        @pl.when(j >= half_b)
-        def _():
-            low = jnp.where(j == half_b, 0, j - 2)
-
-            @pl.loop(0, j - 1 - low)
+        @pl.when(j >= turn)
+        def _():
+            low = jnp.where(j == turn, 0, jnp.minimum(j - 2, 2 * (j - turn) + 1))
+            high = jnp.minimum(j - 1, 2 * (j - turn) + 3)
+
+            @pl.loop(0, high - low)
             def _(t):
                 update_1(start_b + low + t)
 
@@ -409,7 +423,10 @@
     def _():
         for item in range(4):
             inverse_c(item, c).wait_send()
-            factor_y(item // 2, item % 2).wait_send()
+
+            @pl.when(jnp.logical_not(first) if item > 1 else True)
+            def _():
+                factor_y(item // 2, item % 2).wait_send()
 
     @pl.when(y == 1)
     def _():

time: 168 us -> 151 us (0.90)
  Pallas kernels: 164 us -> 147 us
    pallas_call x1, Pallas kernels: 164 us -> 147 us  [streamed(): pl.pallas_call(functools.partial(fused, depth), out_shape=jax.ShapeDtypeS...]
where the time goes in v4:
time: 151 us
  Pallas kernels  147 us (97%)
  local copies, waits for them, and re-layouts  4.47 us (3%)
    pallas_call x1, Pallas kernels, streamed(): pl.pallas_call(functools.partial(fused, depth), out_shape=jax.ShapeDtypeS...  147 us
    unnamed x1, local copies, waits for them, and re-layouts  4.47 us

profile of v4, /device:TPU:29, one launch (start us, length us, event | category | flops | bytes accessed | tf_op | source)
XLA Modules:
  0.0 151.1 jit_solution(17112207402443430810)
XLA Ops:
  0.0 146.6 %shard_map.37 = bf16[4096,512]{1,0:T(8,128)(2,1)} custom-call(bf16[4096,512]{1,0:T(8,128)(2,1)} %m.1, bf16[2,512,1024]{2,1,0:T(8,128)(2,1)} %lo.1, bf16[2,512,1024]{2,1,0:T(8,128)(2,1)} %up.1), custom_call_target="tpu_custom_call" | custom-call | flops 17179869184 | bytes 8388608 | tf_op jit(solution)/shard_map/pallas_call | solution.py:442
  146.7 4.5 %copy.5 = bf16[4096,512]{1,0:T(8,128)(2,1)} copy(bf16[4096,512]{1,0:T(8,128)(2,1)} %shard_map.37) | data formatting | bytes 8388608

commit v5 on v4

--- a/solution.py
+++ b/solution.py
@@ -164,7 +164,7 @@
 
         @pl.when(jnp.logical_not(first) if s == 1 else True)
         def _():
-            act(send(s, b, i, other_c, c_sent.at[0, slot], par))
+            act(send(s, b, i, other_c, c_sent.at[2 * s, slot], par))
 
     def cross_sends(s, b, t, act):
         i = 2 * t + 1 - x
@@ -179,7 +179,7 @@
             def _():
                 act(send(s, b, i, down_z, r_sent.at[slot], own))
 
-        act(send(s, b, i, other_c, c_sent.at[1, slot], par))
+        act(send(s, b, i, other_c, c_sent.at[2 * s + 1, slot], par))
 
     def chain(s, b, begin_b):
         for t in range(2):
@@ -205,12 +205,14 @@
 
             cross_sends(s, b, t, begin)
 
-    def drain(s, last):
+    def drain(s, last, chains, crosses):
         for b in (last - 1, last):
             for t in range(2):
-                chain_sends(s, b, t, finish)
-
-                @pl.when(jnp.logical_not(first) if s == 1 else True)
+                @pl.when(chains)
+                def _():
+                    chain_sends(s, b, t, finish)
+
+                @pl.when(crosses)
                 def _():
                     cross_sends(s, b, t, finish)
 
@@ -360,7 +362,7 @@
         inverse_y(0).start()
         inverse_y(1).start()
 
-        @pl.loop(0, n_a + 4)
+        @pl.loop(0, jnp.where(second, n_a, n_a + 2))
         def _(b):
             phase_a(b, lag)
 
@@ -374,9 +376,10 @@
         factor_y(0, 0).wait_recv()
         factor_y(0, 1).wait_recv()
 
-    drain(0, n_a - 1)
+    eager = both(second, y == 1)
+    drain(0, n_a - 1, True, jnp.logical_not(eager))
     half_b = n_b // 2
-    turn = half_b + y
+    turn = jnp.where(second, n_b, half_b + y)
     lag_b = jnp.where(second, 0, 2)
 
     @pl.loop(0, n_b + 2)
@@ -397,6 +400,10 @@
         def _():
             cross(1, b - lag_b, start_b)
 
+        @pl.when(both(eager, j < 4))
+        def _():
+            cross(0, n_a - 4 + j, 0)
+
         @pl.when(both(j < half_b, jnp.logical_not(second)))
         def _():
             @pl.loop(0, 2)
@@ -413,11 +420,15 @@
             low = jnp.where(j == turn, 0, jnp.minimum(j - 2, 2 * (j - turn) + 1))
             high = jnp.minimum(j - 1, 2 * (j - turn) + 3)
 
+            low = jnp.where(second, 0, low)
+            high = jnp.where(second, jnp.where(j == n_b, n_b, 0), high)
+
             @pl.loop(0, high - low)
             def _(t):
                 update_1(start_b + low + t)
 
-    drain(1, n_a - 1)
+    drain(0, n_a - 1, False, eager)
+    drain(1, n_a - 1, True, jnp.logical_not(first))
 
     @pl.when(y == 0)
     def _():
@@ -454,7 +465,7 @@
             dma((STEPS, chunks)),
             dma((PER,)),
             dma((PER,)),
-            dma((2, PER)),
+            dma((2 * STEPS, PER)),
             dma((PER,)),
             dma((4,)),
             dma((4,)),

time: 151 us -> 139 us (0.921)
  Pallas kernels: 147 us -> 134 us
    pallas_call x1, Pallas kernels: 147 us -> 134 us  [streamed(): pl.pallas_call(functools.partial(fused, depth), out_shape=jax.ShapeDtypeS...]
where the time goes in v5:
time: 139 us
  Pallas kernels  134 us (96%)
  local copies, waits for them, and re-layouts  4.47 us (3%)
    pallas_call x1, Pallas kernels, streamed(): pl.pallas_call(functools.partial(fused, depth), out_shape=jax.ShapeDtypeS...  134 us
    unnamed x1, local copies, waits for them, and re-layouts  4.47 us

profile of v5, /device:TPU:29, one launch (start us, length us, event | category | flops | bytes accessed | tf_op | source)
XLA Modules:
  0.0 138.7 jit_solution(6443013321026594510)
XLA Ops:
  0.0 134.2 %shard_map.37 = bf16[4096,512]{1,0:T(8,128)(2,1)} custom-call(bf16[4096,512]{1,0:T(8,128)(2,1)} %m.1, bf16[2,512,1024]{2,1,0:T(8,128)(2,1)} %lo.1, bf16[2,512,1024]{2,1,0:T(8,128)(2,1)} %up.1), custom_call_target="tpu_custom_call" | custom-call | flops 17179869184 | bytes 8388608 | tf_op jit(solution)/shard_map/pallas_call | solution.py:453
  134.2 4.5 %copy.5 = bf16[4096,512]{1,0:T(8,128)(2,1)} copy(bf16[4096,512]{1,0:T(8,128)(2,1)} %shard_map.37) | data formatting | bytes 8388608
